TPU v7x, 512 devices: a whole 4x4x16 slice. The times are simulated.
512 devices in a mesh: inst: 64 (over x_hi, z, core), tp: 8 (over x_lo, y).
Axes of the slice: x: 4 (x_hi: 2, x_lo: 2; x = x_hi * 2 + x_lo), y: 4, z: 16, core: 2. Of those that a mesh axis runs over, the one named last changes fastest.
Arguments:
- queries: bfloat16 [8192, 8192], P('inst', 'tp'), may hold values from -12 to 12
- span_keys: bfloat16 [8192, 1024], P('inst', 'tp'), may hold values from -12 to 12
- span_values: bfloat16 [8192, 1024], P('inst', 'tp'), may hold values from -6 to 6
- prefix_keys: bfloat16 [4096, 1024], P(('inst', 'tp')), may hold values from -6 to 6
- prefix_values: bfloat16 [4096, 1024], P(('inst', 'tp')), may hold values from -6 to 6
- span_seg: int32 [8192], replicated, may hold values from 0 to 3, never falling along the last dimension, each value on 1 to 4096 neighbouring positions
- prefix_lengths: int32 [4], replicated, may hold values from 1 to 2048, 4096 in all
Outputs:
- attended: bfloat16 [8192, 8192], P('inst', 'tp')
Inputs may be any that keep to these rules, and one draw needn't show every extreme that they name: `span_seg`: requests in order along the block, never falling; each of the 4 requests has 1 to 4096 tokens and one has exactly 4096. `prefix_lengths`: the prefixes lie end to end in request order and sum to 4096; one has exactly 2048.
All inputs are finite; a program needn't handle non-finite values.
Results may differ from a plain program's by a relative error of at most 0.0085.
Values may be sent and summed in bfloat16 or wider, within the bound.
No kernel may reach another device: no remote copies, remote signals or barrier semaphores. Data moves between devices by JAX's collectives and lax.ppermute only.
A program may use at most 128 MiB of HBM per device.

v0:
```python
import functools
import math

import jax
import jax.numpy as jnp
from jax import lax
from jax.experimental import pallas as pl
from jax.experimental.pallas import tpu as pltpu
from jax.sharding import Mesh, PartitionSpec as P

HEADS = 64
KV_HEADS = 8
HD = 128
GROUP = HEADS // KV_HEADS
REQ = 4
SPAN = 8192
PREFIX = 4096
XH, Z, CORE, TP = 2, 16, 2, 8
CHIPS = XH * Z
INST = ("xh", "z", "core")
ROWS = SPAN // (CHIPS * CORE)
KEYS = ROWS * CORE
PIECE = PREFIX // CHIPS
BLOCK_KEYS = KEYS + PIECE
LANES = 2 * ROWS
PARTS = GROUP * ROWS // LANES
STEPS = Z // 2
STATE_ROWS = HD + 8
LOW = -1e30
EXP2_SCALE = math.log2(math.e) / math.sqrt(HD)

SMEM = pl.BlockSpec(memory_space=pltpu.SMEM)
VMEM = pl.BlockSpec(memory_space=pltpu.VMEM)
PARAMS = pltpu.CompilerParams(vmem_limit_bytes=24 * 1024 * 1024)


def turn(tile):
    return tile.astype(jnp.float32).T.astype(jnp.bfloat16)


def pack(place_ref, own_ref, sib_ref, across_ref, diagonal_ref, pre_ref, *block_refs):
    same_xh = [place_ref[0] == xh for xh in range(XH)]
    same_core = [place_ref[2] == core for core in range(CORE)]
    for xh in range(XH):
        for core in range(CORE):
            tiles = []
            for i in range(2):
                near = jnp.where(same_core[core], own_ref[i], sib_ref[i])
                far = jnp.where(same_core[core], across_ref[i], diagonal_ref[i])
                tiles.append(jnp.where(same_xh[xh], near, far))
            block_refs[xh][core * ROWS : (core + 1) * ROWS, :] = tiles[0]
            block_refs[xh][BLOCK_KEYS + core * HD : BLOCK_KEYS + (core + 1) * HD, :] = turn(tiles[1])
        block_refs[xh][KEYS:BLOCK_KEYS, :] = pre_ref[xh * PIECE : (xh + 1) * PIECE, :HD]
        block_refs[xh][BLOCK_KEYS + KEYS :, :] = turn(pre_ref[xh * PIECE : (xh + 1) * PIECE, HD:])


def plan(place_ref, lengths_ref, seg_ref, q_ref, sib_ref, scalars_ref, bounds_ref, rows_ref):
    inst = (place_ref[0] * Z + place_ref[1]) * CORE + place_ref[2]
    sibling = inst + 1 - 2 * place_ref[2]
    seg = seg_ref[...]
    counts = [jnp.int32(0)] + [
        jnp.sum(jnp.where(seg < s, 1.0, 0.0)).astype(jnp.int32) for s in range(1, REQ)
    ]
    starts, ends, running = [], [], jnp.int32(0)
    for s in range(REQ):
        starts.append(running)
        running = running + lengths_ref[s]
        ends.append(running)

    def pick(values, s):
        out = values[0]
        for k in range(1, REQ):
            out = jnp.where(s == k, values[k], out)
        return out

    for half, block in enumerate((inst, sibling)):
        first = block * ROWS
        first_seg, last_seg = jnp.int32(0), jnp.int32(0)
        for s in range(1, REQ):
            first_seg = first_seg + (first >= counts[s]).astype(jnp.int32)
            last_seg = last_seg + (first + ROWS - 1 >= counts[s]).astype(jnp.int32)
        values = (
            pick(starts, first_seg), pick(ends, last_seg), pick(starts, last_seg), pick(ends, first_seg),
            pick(counts, first_seg), first + ROWS, pick(counts, last_seg), first + 1,
        )
        for i, value in enumerate(values):
            scalars_ref[half * 8 + i] = value
        position = first + lax.broadcasted_iota(jnp.int32, (1, ROWS), 1)
        row_seg = jnp.zeros((1, ROWS), jnp.int32)
        for s in range(1, REQ):
            row_seg = row_seg + jnp.where(position >= counts[s], 1, 0)
        bounds_ref[half, 0:1, :] = pick(starts, row_seg)
        bounds_ref[half, 1:2, :] = pick(ends, row_seg)
        bounds_ref[half, 2:3, :] = pick(counts, row_seg)
        bounds_ref[half, 3:4, :] = position + 1
        ref = (q_ref, sib_ref)[half]
        for h in range(GROUP):
            rows_ref[half, h // 2, :, h % 2 * ROWS : (h % 2 + 1) * ROWS] = turn(ref[:, h * HD : (h + 1) * HD])


def absorb_step(step, which, place_ref, scalars_ref, bounds_ref, rows_ref, block_ref, *refs):
    core, z = place_ref[2], place_ref[1]
    origin = lax.rem(jnp.where(core == 0, z - step + Z, z + step), Z)
    xh = core if which is None else which
    final = step == STEPS
    if final:
        _, state, own_ref, sib_ref = refs
    else:
        state = refs[-1]
    if step == 0:
        state[:, :, :HD, :] = jnp.zeros((CORE, PARTS, HD, LANES), jnp.float32)
        state[:, :, HD:, :] = jnp.zeros((CORE, PARTS, STATE_ROWS - HD, LANES), jnp.float32)
        state[:, :, HD : HD + 1, :] = jnp.full((CORE, PARTS, 1, LANES), LOW, jnp.float32)

    def absorb(half, row, count, base, kind, masked):
        keys = block_ref[row : row + count, :]
        vals = jnp.concatenate(
            [block_ref[BLOCK_KEYS + i : BLOCK_KEYS + i + HD, :] for i in range(row, row + count, HD)], axis=1
        )
        every = range(PARTS)
        scores = [jnp.dot(keys, rows_ref[half, b], preferred_element_type=jnp.float32) for b in every]
        if masked:
            index = base + lax.broadcasted_iota(jnp.int32, (count, ROWS), 0)
            low = bounds_ref[half, 2 * kind : 2 * kind + 1, :]
            high = bounds_ref[half, 2 * kind + 1 : 2 * kind + 2, :]
            bias = jnp.where((index >= low) & (index < high), 0.0, LOW)
            bias = jnp.concatenate([bias] * (LANES // ROWS), axis=1)
            scores = [scores[b] + bias for b in every]
        old = [state[half, b, HD : HD + 1, :] for b in every]
        new = [jnp.maximum(old[b], jnp.max(scores[b], axis=0, keepdims=True)) for b in every]
        factor = [jnp.exp2((old[b] - new[b]) * EXP2_SCALE) for b in every]
        expo = [jnp.exp2((scores[b] - new[b]) * EXP2_SCALE) for b in every]
        total = [
            state[half, b, HD + 1 : HD + 2, :] * factor[b] + jnp.sum(expo[b], axis=0, keepdims=True) for b in every
        ]
        summed = [
            state[half, b, :HD, :] * factor[b]
            + jnp.dot(vals, expo[b].astype(jnp.bfloat16), preferred_element_type=jnp.float32)
            for b in every
        ]
        for b in every:
            state[half, b, :HD, :] = summed[b]
            state[half, b, HD : HD + 1, :] = new[b]
            state[half, b, HD + 1 : HD + 2, :] = total[b]

    def visit(half, row, count, base, kind):
        least_lo, most_hi, most_lo, least_hi = [scalars_ref[half * 8 + kind * 4 + i] for i in range(4)]
        seen = (base < most_hi) & (base + count > least_lo)
        whole = (base >= most_lo) & (base + count <= least_hi)

        @pl.when(seen & whole)
        def _():
            absorb(half, row, count, base, kind, False)

        @pl.when(seen & jnp.logical_not(whole))
        def _():
            absorb(half, row, count, base, kind, True)

    def one_half(half, carry):
        visit(half, 0, KEYS, (xh * Z + origin) * KEYS, 1)
        visit(half, KEYS, PIECE, (xh * Z + origin) * PIECE, 0)
        return carry

    lax.fori_loop(0, CORE, one_half, 0)
    if final:
        own_ref[...] = state[0]
        sib_ref[...] = state[1]


def merge(own_ref, other_ref, out_ref):
    for b in range(PARTS):
        top_a, top_b = own_ref[b, HD : HD + 1, :], other_ref[b, HD : HD + 1, :]
        top = jnp.maximum(top_a, top_b)
        factor_a = jnp.exp2((top_a - top) * EXP2_SCALE)
        factor_b = jnp.exp2((top_b - top) * EXP2_SCALE)
        total = own_ref[b, HD + 1 : HD + 2, :] * factor_a + other_ref[b, HD + 1 : HD + 2, :] * factor_b
        result = (own_ref[b, :HD, :] * factor_a + other_ref[b, :HD, :] * factor_b) / total
        for i in range(LANES // ROWS):
            h = b * (LANES // ROWS) + i
            out_ref[:, h * HD : (h + 1) * HD] = result[:, i * ROWS : (i + 1) * ROWS].T.astype(jnp.bfloat16)


STATE = jax.ShapeDtypeStruct((CORE, PARTS, STATE_ROWS, LANES), jnp.float32)
HALF_STATE = jax.ShapeDtypeStruct((PARTS, STATE_ROWS, LANES), jnp.float32)


def call_pack(place, *parts):
    return pl.pallas_call(
        pack,
        out_shape=(jax.ShapeDtypeStruct((2 * BLOCK_KEYS, HD), jnp.bfloat16),) * XH,
        in_specs=[SMEM] + [VMEM] * 5,
        out_specs=(VMEM,) * XH,
        compiler_params=PARAMS,
        name="pack",
    )(place, *parts)


def call_plan(place, prefix_lengths, span_seg, queries, sib_queries):
    return pl.pallas_call(
        plan,
        out_shape=(
            jax.ShapeDtypeStruct((CORE * 8,), jnp.int32),
            jax.ShapeDtypeStruct((CORE, 8, ROWS), jnp.int32),
            jax.ShapeDtypeStruct((CORE, PARTS, HD, LANES), jnp.bfloat16),
        ),
        in_specs=[SMEM, SMEM, VMEM, VMEM, VMEM],
        out_specs=(SMEM, VMEM, VMEM),
        compiler_params=PARAMS,
        name="plan",
    )(place, prefix_lengths, span_seg.reshape(-1, ROWS), queries, sib_queries)


def call_absorb(step, which, place, planned, block, state):
    final = step == STEPS
    return pl.pallas_call(
        functools.partial(absorb_step, step, which),
        out_shape=(STATE, HALF_STATE, HALF_STATE) if final else STATE,
        in_specs=[SMEM, SMEM, VMEM, VMEM, VMEM] + ([VMEM] if step else []),
        out_specs=(VMEM,) * 3 if final else VMEM,
        input_output_aliases={5: 0} if step else {},
        compiler_params=PARAMS,
        cost_estimate=pl.CostEstimate(flops=400_000_000, bytes_accessed=2_000_000, transcendentals=790_000),
        name="absorb",
    )(place, *planned, block, *([state] if step else []))


def call_merge(own, other):
    return pl.pallas_call(
        merge,
        out_shape=jax.ShapeDtypeStruct((ROWS, GROUP * HD), jnp.bfloat16),
        in_specs=[VMEM, VMEM],
        out_specs=VMEM,
        compiler_params=PARAMS,
        name="merge",
    )(own, other)


def at(xh, z, core):
    return (xh * Z + z) * CORE + core


def body(queries, span_keys, span_values, prefix_keys, prefix_values, span_seg, prefix_lengths):
    place = jnp.stack([lax.axis_index(a) for a in INST]).astype(jnp.int32)
    everyone = [(xh, z, c) for xh in range(XH) for z in range(Z) for c in range(CORE)]
    sibling = [(at(xh, z, c), at(xh, z, 1 - c)) for xh, z, c in everyone]
    across = [(at(xh, z, c), at(1 - xh, z, c)) for xh, z, c in everyone]
    diagonal = [(at(xh, z, c), at(1 - xh, z, 1 - c)) for xh, z, c in everyone]
    along = [(at(xh, z, c), at(xh, (z + 1 - 2 * c) % Z, c)) for xh, z, c in everyone]

    pre = jnp.concatenate(
        [prefix_keys.reshape(-1, KV_HEADS, HD), prefix_values.reshape(-1, KV_HEADS, HD)], axis=2
    ).transpose(1, 0, 2)
    pre = jnp.broadcast_to(pre[None], (XH * CORE,) + pre.shape).reshape((XH * CORE * TP,) + pre.shape[1:])
    pre = lax.all_to_all(pre, ("xh", "core", "tp"), split_axis=0, concat_axis=0, tiled=True)
    pre = pre.reshape(XH * PIECE, 2 * HD)

    span = jnp.stack([span_keys, span_values])
    spans = [span] + [lax.ppermute(span, INST, way) for way in (sibling, across, diagonal)]
    blocks = list(call_pack(place, *spans, pre))
    planned = call_plan(place, prefix_lengths, span_seg, queries, lax.ppermute(queries, INST, sibling))

    mine = jnp.where(place[2] == 0, blocks[0], blocks[1])
    blocks = [lax.ppermute(block, INST, along) for block in blocks]
    state = call_absorb(0, None, place, planned, mine, None)
    for step in range(1, STEPS):
        for xh in range(XH):
            block, state = lax.optimization_barrier((blocks[xh], state))
            if step < STEPS - 1:
                blocks[xh] = lax.ppermute(block, INST, along)
            elif xh == 0:
                blocks[xh] = block
            else:
                mine = jnp.where(place[2] == 0, blocks[0], block)
                mine = lax.ppermute(mine, INST, along)
            state = call_absorb(step, xh, place, planned, block, state)
    _, own, sib = call_absorb(STEPS, None, place, planned, *lax.optimization_barrier((mine, state)))
    return call_merge(own, lax.ppermute(sib, INST, sibling))


def solution(mesh):
    cut = Mesh(mesh.devices.reshape(XH, Z, CORE, TP), INST + ("tp",))
    in_specs = (
        P(INST, "tp"),
        P(INST, "tp"),
        P(INST, "tp"),
        P(INST + ("tp",), None),
        P(INST + ("tp",), None),
        P(),
        P(),
    )
    return jax.shard_map(body, mesh=cut, in_specs=in_specs, out_specs=P(INST, "tp"), check_vma=False)
```

profile of v0, /device:TPU:1, one launch (start us, length us, event | category | flops | bytes accessed | tf_op | source)
XLA Modules:
  0.0 114.5 jit_solution(16590879170865649376)
XLA Ops:
  1.5 10.4 %all-to-all-start = ((bf16[32,8,256]{2,1,0:T(8,128)(2,1)}), bf16[32,8,256]{2,1,0:T(8,128)(2,1)S(1)}, u32[]{:S(2)}, u32[]{:S(2)}) async-start(bf16[32,8,256]{2,1,0:T(8,128)(2,1)} %bitcast.9), calls=%async_computation | async-start | bytes 262144 | tf_op jit(solution)/shard_map/all_to_all | solution.py:254
  11.9 0.8 pad_maximum_fusion.own_ref
  12.7 5.1 %collective-permute-start.3 = (bf16[2,128,128]{2,1,0:T(8,128)(2,1)S(1)}, bf16[2,128,128]{2,1,0:T(8,128)(2,1)S(1)}, u32[]{:S(2)}, u32[]{:S(2)}) collective-permute-start(bf16[2,128,128]{2,1,0:T(8,128)(2,1)S(1)} %pad_maximum_fusion.own_ref), channel_id=1, source_target_pairs={{0,264},{8,256},{16,280},{24,272},{32,296},{40,288},{48,312},{56,3... | collective-permute-start | bytes 196616 | tf_op jit(solution)/shard_map/ppermute | solution.py:258
  17.8 1.9 %collective-permute-start.2 = (bf16[2,128,128]{2,1,0:T(8,128)(2,1)S(1)}, bf16[2,128,128]{2,1,0:T(8,128)(2,1)S(1)}, u32[]{:S(2)}, u32[]{:S(2)}) collective-permute-start(bf16[2,128,128]{2,1,0:T(8,128)(2,1)S(1)} %pad_maximum_fusion.own_ref), channel_id=1, source_target_pairs={{0,256},{8,264},{16,272},{24,280},{32,288},{40,296},{48,304},{56,3... | collective-permute-start | bytes 196616 | tf_op jit(solution)/shard_map/ppermute | solution.py:258
  19.7 2.4 %collective-permute-start.1 = (bf16[2,128,128]{2,1,0:T(8,128)(2,1)S(1)}, bf16[2,128,128]{2,1,0:T(8,128)(2,1)S(1)}, u32[]{:S(2)}, u32[]{:S(2)}) collective-permute-start(bf16[2,128,128]{2,1,0:T(8,128)(2,1)S(1)} %pad_maximum_fusion.own_ref), channel_id=1, source_target_pairs={{0,8},{8,0},{16,24},{24,16},{32,40},{40,32},{48,56},{56,48},{64,72... | collective-permute-start | bytes 196616 | tf_op jit(solution)/shard_map/ppermute | solution.py:258
  22.1 2.0 %collective-permute-start = (bf16[128,1024]{1,0:T(8,128)(2,1)}, bf16[128,1024]{1,0:T(8,128)(2,1)S(1)}, u32[]{:S(2)}, u32[]{:S(2)}) collective-permute-start(bf16[128,1024]{1,0:T(8,128)(2,1)} %q_ref.1), channel_id=1, source_target_pairs={{0,8},{8,0},{16,24},{24,16},{32,40},{40,32},{48,56},{56,48},{64,72... | collective-permute-start | bytes 786440 | tf_op jit(solution)/shard_map/ppermute | solution.py:260
  25.4 9.2 %collective-permute-start.4 = (bf16[768,128]{1,0:T(8,128)(2,1)S(1)}, bf16[768,128]{1,0:T(8,128)(2,1)S(1)}, u32[]{:S(2)}, u32[]{:S(2)}) collective-permute-start(bf16[768,128]{1,0:T(8,128)(2,1)S(1)} %get-tuple-element.45), channel_id=1, source_target_pairs={{0,16},{8,248},{16,32},{24,8},{32,48},{40,24},{48,64},{56,40},{64,... | collective-permute-start | bytes 589832 | tf_op jit(solution)/shard_map/ppermute | solution.py:263
  34.7 2.6 %collective-permute-start.6 = (bf16[768,128]{1,0:T(8,128)(2,1)S(1)}, bf16[768,128]{1,0:T(8,128)(2,1)S(1)}, u32[]{:S(2)}, u32[]{:S(2)}) collective-permute-start(bf16[768,128]{1,0:T(8,128)(2,1)S(1)} %get-tuple-element.46), channel_id=1, source_target_pairs={{0,16},{8,248},{16,32},{24,8},{32,48},{40,24},{48,64},{56,40},{64,... | collective-permute-start | bytes 589832 | tf_op jit(solution)/shard_map/ppermute | solution.py:263
  37.4 1.3 %plan.1 = (s32[16]{0:T(128)S(1)}, s32[2,8,128]{2,1,0:T(8,128)S(1)}, bf16[2,4,128,256]{3,2,1,0:T(8,128)(2,1)S(1)}) custom-call(s32[3]{0:T(128)S(1)} %pad_add_fusion.place_ref, s32[4]{0:T(128)S(1)} %copy-done.2, s32[64,128]{1,0:T(8,128)S(1)} %bitcast.13, bf16[128,1024]{1,0:T(8,128)(2,1)S(1)} %copy-done, bf16[128,1024]{1,0:T(8,128)(2,1)S(1)} %collective-permute-done.sib_ref), custom_call_target="tpu_custom_call" | custom-call | tf_op jit(solution)/shard_map/plan/pallas_call | solution.py:199
  39.4 2.9 %collective-permute-start.5 = (bf16[768,128]{1,0:T(8,128)(2,1)S(1)}, bf16[768,128]{1,0:T(8,128)(2,1)S(1)}, u32[]{:S(2)}, u32[]{:S(2)}) collective-permute-start(bf16[768,128]{1,0:T(8,128)(2,1)S(1)} %collective-permute-done.4.block_ref), channel_id=1, source_target_pairs={{0,16},{8,248},{16,32},{24,8},{32,48},{40,24},{48,64},{56,40},{64,... | collective-permute-start | bytes 589832 | tf_op jit(solution)/shard_map/ppermute | solution.py:269
  42.3 1.5 %absorb.17.refs_0_ = f32[2,4,136,256]{3,2,1,0:T(8,128)S(1)} custom-call(s32[3]{0:T(128)S(1)} %pad_add_fusion.place_ref, s32[16]{0:T(128)S(1)} %get-tuple-element.42.scalars_ref, s32[2,8,128]{2,1,0:T(8,128)S(1)} %get-tuple-element.43.bounds_ref, bf16[2,4,128,256]{3,2,1,0:T(8,128)(2,1)S(1)} %get-tuple-element.44.rows_ref, ...), custom_call_target="tpu_custom_call", output_to_operand_aliasing={{}: (5, {})} | custom-call | flops 400000000 | bytes 2000000 | tf_op jit(solution)/shard_map/absorb/pallas_call | solution.py:215
  43.8 1.9 %collective-permute-start.8 = (bf16[768,128]{1,0:T(8,128)(2,1)S(1)}, bf16[768,128]{1,0:T(8,128)(2,1)S(1)}, u32[]{:S(2)}, u32[]{:S(2)}) collective-permute-start(bf16[768,128]{1,0:T(8,128)(2,1)S(1)} %collective-permute-done.6.block_ref), channel_id=1, source_target_pairs={{0,16},{8,248},{16,32},{24,8},{32,48},{40,24},{48,64},{56,40},{64,... | collective-permute-start | bytes 589832 | tf_op jit(solution)/shard_map/ppermute | solution.py:269
  46.4 4.3 %collective-permute-start.7 = (bf16[768,128]{1,0:T(8,128)(2,1)S(1)}, bf16[768,128]{1,0:T(8,128)(2,1)S(1)}, u32[]{:S(2)}, u32[]{:S(2)}) collective-permute-start(bf16[768,128]{1,0:T(8,128)(2,1)S(1)} %collective-permute-done.5.block_ref), channel_id=1, source_target_pairs={{0,16},{8,248},{16,32},{24,8},{32,48},{40,24},{48,64},{56,40},{64,... | collective-permute-start | bytes 589832 | tf_op jit(solution)/shard_map/ppermute | solution.py:269
  50.8 1.5 %absorb.19.refs_0_ = f32[2,4,136,256]{3,2,1,0:T(8,128)S(1)} custom-call(s32[3]{0:T(128)S(1)} %pad_add_fusion.place_ref, s32[16]{0:T(128)S(1)} %get-tuple-element.42.scalars_ref, s32[2,8,128]{2,1,0:T(8,128)S(1)} %get-tuple-element.43.bounds_ref, bf16[2,4,128,256]{3,2,1,0:T(8,128)(2,1)S(1)} %get-tuple-element.44.rows_ref, ...), custom_call_target="tpu_custom_call", output_to_operand_aliasing={{}: (5, {})} | custom-call | flops 400000000 | bytes 2000000 | tf_op jit(solution)/shard_map/absorb/pallas_call | solution.py:215
  52.3 1.9 %collective-permute-start.10 = (bf16[768,128]{1,0:T(8,128)(2,1)S(1)}, bf16[768,128]{1,0:T(8,128)(2,1)S(1)}, u32[]{:S(2)}, u32[]{:S(2)}) collective-permute-start(bf16[768,128]{1,0:T(8,128)(2,1)S(1)} %collective-permute-done.8.block_ref), channel_id=1, source_target_pairs={{0,16},{8,248},{16,32},{24,8},{32,48},{40,24},{48,64},{56,40},{64,... | collective-permute-start | bytes 589832 | tf_op jit(solution)/shard_map/ppermute | solution.py:269
  54.9 3.6 %collective-permute-start.9 = (bf16[768,128]{1,0:T(8,128)(2,1)S(1)}, bf16[768,128]{1,0:T(8,128)(2,1)S(1)}, u32[]{:S(2)}, u32[]{:S(2)}) collective-permute-start(bf16[768,128]{1,0:T(8,128)(2,1)S(1)} %collective-permute-done.7.block_ref), channel_id=1, source_target_pairs={{0,16},{8,248},{16,32},{24,8},{32,48},{40,24},{48,64},{56,40},{64,... | collective-permute-start | bytes 589832 | tf_op jit(solution)/shard_map/ppermute | solution.py:269
  58.5 1.5 %absorb.21.refs_0_ = f32[2,4,136,256]{3,2,1,0:T(8,128)S(1)} custom-call(s32[3]{0:T(128)S(1)} %pad_add_fusion.place_ref, s32[16]{0:T(128)S(1)} %get-tuple-element.42.scalars_ref, s32[2,8,128]{2,1,0:T(8,128)S(1)} %get-tuple-element.43.bounds_ref, bf16[2,4,128,256]{3,2,1,0:T(8,128)(2,1)S(1)} %get-tuple-element.44.rows_ref, ...), custom_call_target="tpu_custom_call", output_to_operand_aliasing={{}: (5, {})} | custom-call | flops 400000000 | bytes 2000000 | tf_op jit(solution)/shard_map/absorb/pallas_call | solution.py:215
  60.1 1.9 %collective-permute-start.12 = (bf16[768,128]{1,0:T(8,128)(2,1)S(1)}, bf16[768,128]{1,0:T(8,128)(2,1)S(1)}, u32[]{:S(2)}, u32[]{:S(2)}) collective-permute-start(bf16[768,128]{1,0:T(8,128)(2,1)S(1)} %collective-permute-done.10.block_ref), channel_id=1, source_target_pairs={{0,16},{8,248},{16,32},{24,8},{32,48},{40,24},{48,64},{56,40},{64,... | collective-permute-start | bytes 589832 | tf_op jit(solution)/shard_map/ppermute | solution.py:269
  62.7 3.3 %collective-permute-start.11 = (bf16[768,128]{1,0:T(8,128)(2,1)S(1)}, bf16[768,128]{1,0:T(8,128)(2,1)S(1)}, u32[]{:S(2)}, u32[]{:S(2)}) collective-permute-start(bf16[768,128]{1,0:T(8,128)(2,1)S(1)} %collective-permute-done.9.block_ref), channel_id=1, source_target_pairs={{0,16},{8,248},{16,32},{24,8},{32,48},{40,24},{48,64},{56,40},{64,... | collective-permute-start | bytes 589832 | tf_op jit(solution)/shard_map/ppermute | solution.py:269
  66.0 1.6 %absorb.23.refs_0_ = f32[2,4,136,256]{3,2,1,0:T(8,128)S(1)} custom-call(s32[3]{0:T(128)S(1)} %pad_add_fusion.place_ref, s32[16]{0:T(128)S(1)} %get-tuple-element.42.scalars_ref, s32[2,8,128]{2,1,0:T(8,128)S(1)} %get-tuple-element.43.bounds_ref, bf16[2,4,128,256]{3,2,1,0:T(8,128)(2,1)S(1)} %get-tuple-element.44.rows_ref, ...), custom_call_target="tpu_custom_call", output_to_operand_aliasing={{}: (5, {})} | custom-call | flops 400000000 | bytes 2000000 | tf_op jit(solution)/shard_map/absorb/pallas_call | solution.py:215
  67.6 2.1 %collective-permute-start.14 = (bf16[768,128]{1,0:T(8,128)(2,1)S(1)}, bf16[768,128]{1,0:T(8,128)(2,1)S(1)}, u32[]{:S(2)}, u32[]{:S(2)}) collective-permute-start(bf16[768,128]{1,0:T(8,128)(2,1)S(1)} %collective-permute-done.12.block_ref), channel_id=1, source_target_pairs={{0,16},{8,248},{16,32},{24,8},{32,48},{40,24},{48,64},{56,40},{64,... | collective-permute-start | bytes 589832 | tf_op jit(solution)/shard_map/ppermute | solution.py:269
  70.3 3.3 %collective-permute-start.13 = (bf16[768,128]{1,0:T(8,128)(2,1)S(1)}, bf16[768,128]{1,0:T(8,128)(2,1)S(1)}, u32[]{:S(2)}, u32[]{:S(2)}) collective-permute-start(bf16[768,128]{1,0:T(8,128)(2,1)S(1)} %collective-permute-done.11.block_ref), channel_id=1, source_target_pairs={{0,16},{8,248},{16,32},{24,8},{32,48},{40,24},{48,64},{56,40},{64,... | collective-permute-start | bytes 589832 | tf_op jit(solution)/shard_map/ppermute | solution.py:269
  73.6 1.6 %absorb.25.refs_0_ = f32[2,4,136,256]{3,2,1,0:T(8,128)S(1)} custom-call(s32[3]{0:T(128)S(1)} %pad_add_fusion.place_ref, s32[16]{0:T(128)S(1)} %get-tuple-element.42.scalars_ref, s32[2,8,128]{2,1,0:T(8,128)S(1)} %get-tuple-element.43.bounds_ref, bf16[2,4,128,256]{3,2,1,0:T(8,128)(2,1)S(1)} %get-tuple-element.44.rows_ref, ...), custom_call_target="tpu_custom_call", output_to_operand_aliasing={{}: (5, {})} | custom-call | flops 400000000 | bytes 2000000 | tf_op jit(solution)/shard_map/absorb/pallas_call | solution.py:215
  75.2 2.1 %collective-permute-start.16 = (bf16[768,128]{1,0:T(8,128)(2,1)S(1)}, bf16[768,128]{1,0:T(8,128)(2,1)S(1)}, u32[]{:S(2)}, u32[]{:S(2)}) collective-permute-start(bf16[768,128]{1,0:T(8,128)(2,1)S(1)} %collective-permute-done.14.block_ref), channel_id=1, source_target_pairs={{0,16},{8,248},{16,32},{24,8},{32,48},{40,24},{48,64},{56,40},{64,... | collective-permute-start | bytes 589832 | tf_op jit(solution)/shard_map/ppermute | solution.py:269
  77.9 3.5 %collective-permute-start.15 = (bf16[768,128]{1,0:T(8,128)(2,1)S(1)}, bf16[768,128]{1,0:T(8,128)(2,1)S(1)}, u32[]{:S(2)}, u32[]{:S(2)}) collective-permute-start(bf16[768,128]{1,0:T(8,128)(2,1)S(1)} %collective-permute-done.13.block_ref), channel_id=1, source_target_pairs={{0,16},{8,248},{16,32},{24,8},{32,48},{40,24},{48,64},{56,40},{64,... | collective-permute-start | bytes 589832 | tf_op jit(solution)/shard_map/ppermute | solution.py:269
  82.1 2.8 %collective-permute-start.17 = (bf16[768,128]{1,0:T(8,128)(2,1)S(1)}, bf16[768,128]{1,0:T(8,128)(2,1)S(1)}, u32[]{:S(2)}, u32[]{:S(2)}) collective-permute-start(bf16[768,128]{1,0:T(8,128)(2,1)S(1)} %collective-permute-done.16.block_ref), channel_id=1, source_target_pairs={{0,16},{8,248},{16,32},{24,8},{32,48},{40,24},{48,64},{56,40},{64,... | collective-permute-start | bytes 589832 | tf_op jit(solution)/shard_map/ppermute | solution.py:269
  86.2 2.3 %collective-permute-done.17.block_ref = bf16[768,128]{1,0:T(8,128)(2,1)S(1)} collective-permute-done((bf16[768,128]{1,0:T(8,128)(2,1)S(1)}, bf16[768,128]{1,0:T(8,128)(2,1)S(1)}, u32[]{:S(2)}, u32[]{:S(2)}) %collective-permute-start.17) | collective-permute-done | bytes 196640 | tf_op jit(solution)/shard_map/ppermute | solution.py:269
  88.5 4.0 %collective-permute-start.18 = (bf16[768,128]{1,0:T(8,128)(2,1)S(1)}, bf16[768,128]{1,0:T(8,128)(2,1)S(1)}, u32[]{:S(2)}, u32[]{:S(2)}) collective-permute-start(bf16[768,128]{1,0:T(8,128)(2,1)S(1)} %broadcast_select_fusion), channel_id=1, source_target_pairs={{0,16},{8,248},{16,32},{24,8},{32,48},{40,24},{48,64},{56,40},{64,... | collective-permute-start | bytes 589832 | tf_op jit(solution)/shard_map/ppermute | solution.py:274
  93.2 2.1 %collective-permute-done.18.block_ref = bf16[768,128]{1,0:T(8,128)(2,1)S(1)} collective-permute-done((bf16[768,128]{1,0:T(8,128)(2,1)S(1)}, bf16[768,128]{1,0:T(8,128)(2,1)S(1)}, u32[]{:S(2)}, u32[]{:S(2)}) %collective-permute-start.18) | collective-permute-done | bytes 196640 | tf_op jit(solution)/shard_map/ppermute | solution.py:274
  95.9 16.1 %collective-permute-start.19 = (f32[4,136,256]{2,1,0:T(8,128)S(1)}, f32[4,136,256]{2,1,0:T(8,128)S(1)}, u32[]{:S(2)}, u32[]{:S(2)}) collective-permute-start(f32[4,136,256]{2,1,0:T(8,128)S(1)} %get-tuple-element.78), channel_id=1, source_target_pairs={{0,8},{8,0},{16,24},{24,16},{32,40},{40,32},{48,56},{56,48},{64,72... | collective-permute-start | bytes 1671176 | tf_op jit(solution)/shard_map/ppermute | solution.py:277
  112.0 1.6 %collective-permute-done.19.other_ref = f32[4,136,256]{2,1,0:T(8,128)S(1)} collective-permute-done((f32[4,136,256]{2,1,0:T(8,128)S(1)}, f32[4,136,256]{2,1,0:T(8,128)S(1)}, u32[]{:S(2)}, u32[]{:S(2)}) %collective-permute-start.19) | collective-permute-done | bytes 557088 | tf_op jit(solution)/shard_map/ppermute | solution.py:277
  113.6 0.9 merge.1
  (41 shorter events, 10.0 us)
Async XLA Ops:
  0.0 37.3 %copy-start = (bf16[128,1024]{1,0:T(8,128)(2,1)S(1)}, bf16[128,1024]{1,0:T(8,128)(2,1)}, u32[]{:S(2)}) copy-start(bf16[128,1024]{1,0:T(8,128)(2,1)} %q_ref.1) | copy-start | bytes 786436
  0.0 37.4 %copy-start.2 = (s32[4]{0:T(128)S(1)}, s32[4]{0:T(128)}, u32[]{:S(2)}) copy-start(s32[4]{0:T(128)} %lengths_ref.1) | copy-start | bytes 52
  0.0 37.4 %copy-start.1 = (s32[8192]{0:T(1024)S(1)}, s32[8192]{0:T(1024)}, u32[]{:S(2)}) copy-start(s32[8192]{0:T(1024)} %param.12) | copy-start | bytes 98308
  1.5 23.3 %all-to-all-start = ((bf16[32,8,256]{2,1,0:T(8,128)(2,1)}), bf16[32,8,256]{2,1,0:T(8,128)(2,1)S(1)}, u32[]{:S(2)}, u32[]{:S(2)}) async-start(bf16[32,8,256]{2,1,0:T(8,128)(2,1)} %bitcast.9), calls=%async_computation | async-start | bytes 262144 | tf_op jit(solution)/shard_map/all_to_all | solution.py:254
  12.7 11.5 %collective-permute-start.3 = (bf16[2,128,128]{2,1,0:T(8,128)(2,1)S(1)}, bf16[2,128,128]{2,1,0:T(8,128)(2,1)S(1)}, u32[]{:S(2)}, u32[]{:S(2)}) collective-permute-start(bf16[2,128,128]{2,1,0:T(8,128)(2,1)S(1)} %pad_maximum_fusion.own_ref), channel_id=1, source_target_pairs={{0,264},{8,256},{16,280},{24,272},{32,296},{40,288},{48,312},{56,3... | collective-permute-start | bytes 196616 | tf_op jit(solution)/shard_map/ppermute | solution.py:258
  17.8 6.9 %collective-permute-start.2 = (bf16[2,128,128]{2,1,0:T(8,128)(2,1)S(1)}, bf16[2,128,128]{2,1,0:T(8,128)(2,1)S(1)}, u32[]{:S(2)}, u32[]{:S(2)}) collective-permute-start(bf16[2,128,128]{2,1,0:T(8,128)(2,1)S(1)} %pad_maximum_fusion.own_ref), channel_id=1, source_target_pairs={{0,256},{8,264},{16,272},{24,280},{32,288},{40,296},{48,304},{56,3... | collective-permute-start | bytes 196616 | tf_op jit(solution)/shard_map/ppermute | solution.py:258
  19.7 5.0 %collective-permute-start.1 = (bf16[2,128,128]{2,1,0:T(8,128)(2,1)S(1)}, bf16[2,128,128]{2,1,0:T(8,128)(2,1)S(1)}, u32[]{:S(2)}, u32[]{:S(2)}) collective-permute-start(bf16[2,128,128]{2,1,0:T(8,128)(2,1)S(1)} %pad_maximum_fusion.own_ref), channel_id=1, source_target_pairs={{0,8},{8,0},{16,24},{24,16},{32,40},{40,32},{48,56},{56,48},{64,72... | collective-permute-start | bytes 196616 | tf_op jit(solution)/shard_map/ppermute | solution.py:258
  22.1 15.3 %collective-permute-start = (bf16[128,1024]{1,0:T(8,128)(2,1)}, bf16[128,1024]{1,0:T(8,128)(2,1)S(1)}, u32[]{:S(2)}, u32[]{:S(2)}) collective-permute-start(bf16[128,1024]{1,0:T(8,128)(2,1)} %q_ref.1), channel_id=1, source_target_pairs={{0,8},{8,0},{16,24},{24,16},{32,40},{40,32},{48,56},{56,48},{64,72... | collective-permute-start | bytes 786440 | tf_op jit(solution)/shard_map/ppermute | solution.py:260
  25.4 14.0 %collective-permute-start.4 = (bf16[768,128]{1,0:T(8,128)(2,1)S(1)}, bf16[768,128]{1,0:T(8,128)(2,1)S(1)}, u32[]{:S(2)}, u32[]{:S(2)}) collective-permute-start(bf16[768,128]{1,0:T(8,128)(2,1)S(1)} %get-tuple-element.45), channel_id=1, source_target_pairs={{0,16},{8,248},{16,32},{24,8},{32,48},{40,24},{48,64},{56,40},{64,... | collective-permute-start | bytes 589832 | tf_op jit(solution)/shard_map/ppermute | solution.py:263
  34.7 9.2 %collective-permute-start.6 = (bf16[768,128]{1,0:T(8,128)(2,1)S(1)}, bf16[768,128]{1,0:T(8,128)(2,1)S(1)}, u32[]{:S(2)}, u32[]{:S(2)}) collective-permute-start(bf16[768,128]{1,0:T(8,128)(2,1)S(1)} %get-tuple-element.46), channel_id=1, source_target_pairs={{0,16},{8,248},{16,32},{24,8},{32,48},{40,24},{48,64},{56,40},{64,... | collective-permute-start | bytes 589832 | tf_op jit(solution)/shard_map/ppermute | solution.py:263
  39.4 7.0 %collective-permute-start.5 = (bf16[768,128]{1,0:T(8,128)(2,1)S(1)}, bf16[768,128]{1,0:T(8,128)(2,1)S(1)}, u32[]{:S(2)}, u32[]{:S(2)}) collective-permute-start(bf16[768,128]{1,0:T(8,128)(2,1)S(1)} %collective-permute-done.4.block_ref), channel_id=1, source_target_pairs={{0,16},{8,248},{16,32},{24,8},{32,48},{40,24},{48,64},{56,40},{64,... | collective-permute-start | bytes 589832 | tf_op jit(solution)/shard_map/ppermute | solution.py:269
  43.8 8.5 %collective-permute-start.8 = (bf16[768,128]{1,0:T(8,128)(2,1)S(1)}, bf16[768,128]{1,0:T(8,128)(2,1)S(1)}, u32[]{:S(2)}, u32[]{:S(2)}) collective-permute-start(bf16[768,128]{1,0:T(8,128)(2,1)S(1)} %collective-permute-done.6.block_ref), channel_id=1, source_target_pairs={{0,16},{8,248},{16,32},{24,8},{32,48},{40,24},{48,64},{56,40},{64,... | collective-permute-start | bytes 589832 | tf_op jit(solution)/shard_map/ppermute | solution.py:269
  46.4 8.5 %collective-permute-start.7 = (bf16[768,128]{1,0:T(8,128)(2,1)S(1)}, bf16[768,128]{1,0:T(8,128)(2,1)S(1)}, u32[]{:S(2)}, u32[]{:S(2)}) collective-permute-start(bf16[768,128]{1,0:T(8,128)(2,1)S(1)} %collective-permute-done.5.block_ref), channel_id=1, source_target_pairs={{0,16},{8,248},{16,32},{24,8},{32,48},{40,24},{48,64},{56,40},{64,... | collective-permute-start | bytes 589832 | tf_op jit(solution)/shard_map/ppermute | solution.py:269
  52.3 7.8 %collective-permute-start.10 = (bf16[768,128]{1,0:T(8,128)(2,1)S(1)}, bf16[768,128]{1,0:T(8,128)(2,1)S(1)}, u32[]{:S(2)}, u32[]{:S(2)}) collective-permute-start(bf16[768,128]{1,0:T(8,128)(2,1)S(1)} %collective-permute-done.8.block_ref), channel_id=1, source_target_pairs={{0,16},{8,248},{16,32},{24,8},{32,48},{40,24},{48,64},{56,40},{64,... | collective-permute-start | bytes 589832 | tf_op jit(solution)/shard_map/ppermute | solution.py:269
  54.9 7.8 %collective-permute-start.9 = (bf16[768,128]{1,0:T(8,128)(2,1)S(1)}, bf16[768,128]{1,0:T(8,128)(2,1)S(1)}, u32[]{:S(2)}, u32[]{:S(2)}) collective-permute-start(bf16[768,128]{1,0:T(8,128)(2,1)S(1)} %collective-permute-done.7.block_ref), channel_id=1, source_target_pairs={{0,16},{8,248},{16,32},{24,8},{32,48},{40,24},{48,64},{56,40},{64,... | collective-permute-start | bytes 589832 | tf_op jit(solution)/shard_map/ppermute | solution.py:269
  60.1 7.4 %collective-permute-start.12 = (bf16[768,128]{1,0:T(8,128)(2,1)S(1)}, bf16[768,128]{1,0:T(8,128)(2,1)S(1)}, u32[]{:S(2)}, u32[]{:S(2)}) collective-permute-start(bf16[768,128]{1,0:T(8,128)(2,1)S(1)} %collective-permute-done.10.block_ref), channel_id=1, source_target_pairs={{0,16},{8,248},{16,32},{24,8},{32,48},{40,24},{48,64},{56,40},{64,... | collective-permute-start | bytes 589832 | tf_op jit(solution)/shard_map/ppermute | solution.py:269
  62.7 7.6 %collective-permute-start.11 = (bf16[768,128]{1,0:T(8,128)(2,1)S(1)}, bf16[768,128]{1,0:T(8,128)(2,1)S(1)}, u32[]{:S(2)}, u32[]{:S(2)}) collective-permute-start(bf16[768,128]{1,0:T(8,128)(2,1)S(1)} %collective-permute-done.9.block_ref), channel_id=1, source_target_pairs={{0,16},{8,248},{16,32},{24,8},{32,48},{40,24},{48,64},{56,40},{64,... | collective-permute-start | bytes 589832 | tf_op jit(solution)/shard_map/ppermute | solution.py:269
  67.6 7.7 %collective-permute-start.14 = (bf16[768,128]{1,0:T(8,128)(2,1)S(1)}, bf16[768,128]{1,0:T(8,128)(2,1)S(1)}, u32[]{:S(2)}, u32[]{:S(2)}) collective-permute-start(bf16[768,128]{1,0:T(8,128)(2,1)S(1)} %collective-permute-done.12.block_ref), channel_id=1, source_target_pairs={{0,16},{8,248},{16,32},{24,8},{32,48},{40,24},{48,64},{56,40},{64,... | collective-permute-start | bytes 589832 | tf_op jit(solution)/shard_map/ppermute | solution.py:269
  70.3 7.6 %collective-permute-start.13 = (bf16[768,128]{1,0:T(8,128)(2,1)S(1)}, bf16[768,128]{1,0:T(8,128)(2,1)S(1)}, u32[]{:S(2)}, u32[]{:S(2)}) collective-permute-start(bf16[768,128]{1,0:T(8,128)(2,1)S(1)} %collective-permute-done.11.block_ref), channel_id=1, source_target_pairs={{0,16},{8,248},{16,32},{24,8},{32,48},{40,24},{48,64},{56,40},{64,... | collective-permute-start | bytes 589832 | tf_op jit(solution)/shard_map/ppermute | solution.py:269
  75.2 6.9 %collective-permute-start.16 = (bf16[768,128]{1,0:T(8,128)(2,1)S(1)}, bf16[768,128]{1,0:T(8,128)(2,1)S(1)}, u32[]{:S(2)}, u32[]{:S(2)}) collective-permute-start(bf16[768,128]{1,0:T(8,128)(2,1)S(1)} %collective-permute-done.14.block_ref), channel_id=1, source_target_pairs={{0,16},{8,248},{16,32},{24,8},{32,48},{40,24},{48,64},{56,40},{64,... | collective-permute-start | bytes 589832 | tf_op jit(solution)/shard_map/ppermute | solution.py:269
  77.9 7.6 %collective-permute-start.15 = (bf16[768,128]{1,0:T(8,128)(2,1)S(1)}, bf16[768,128]{1,0:T(8,128)(2,1)S(1)}, u32[]{:S(2)}, u32[]{:S(2)}) collective-permute-start(bf16[768,128]{1,0:T(8,128)(2,1)S(1)} %collective-permute-done.13.block_ref), channel_id=1, source_target_pairs={{0,16},{8,248},{16,32},{24,8},{32,48},{40,24},{48,64},{56,40},{64,... | collective-permute-start | bytes 589832 | tf_op jit(solution)/shard_map/ppermute | solution.py:269
  82.1 6.4 %collective-permute-start.17 = (bf16[768,128]{1,0:T(8,128)(2,1)S(1)}, bf16[768,128]{1,0:T(8,128)(2,1)S(1)}, u32[]{:S(2)}, u32[]{:S(2)}) collective-permute-start(bf16[768,128]{1,0:T(8,128)(2,1)S(1)} %collective-permute-done.16.block_ref), channel_id=1, source_target_pairs={{0,16},{8,248},{16,32},{24,8},{32,48},{40,24},{48,64},{56,40},{64,... | collective-permute-start | bytes 589832 | tf_op jit(solution)/shard_map/ppermute | solution.py:269
  88.5 6.7 %collective-permute-start.18 = (bf16[768,128]{1,0:T(8,128)(2,1)S(1)}, bf16[768,128]{1,0:T(8,128)(2,1)S(1)}, u32[]{:S(2)}, u32[]{:S(2)}) collective-permute-start(bf16[768,128]{1,0:T(8,128)(2,1)S(1)} %broadcast_select_fusion), channel_id=1, source_target_pairs={{0,16},{8,248},{16,32},{24,8},{32,48},{40,24},{48,64},{56,40},{64,... | collective-permute-start | bytes 589832 | tf_op jit(solution)/shard_map/ppermute | solution.py:274
  95.9 17.7 %collective-permute-start.19 = (f32[4,136,256]{2,1,0:T(8,128)S(1)}, f32[4,136,256]{2,1,0:T(8,128)S(1)}, u32[]{:S(2)}, u32[]{:S(2)}) collective-permute-start(f32[4,136,256]{2,1,0:T(8,128)S(1)} %get-tuple-element.78), channel_id=1, source_target_pairs={{0,8},{8,0},{16,24},{24,16},{32,40},{40,32},{48,56},{56,48},{64,72... | collective-permute-start | bytes 1671176 | tf_op jit(solution)/shard_map/ppermute | solution.py:277
where the time goes:
time: 115 us; the launch traced here: 114 us
  starting transfers between devices  87.4 us (76%)
  Pallas kernels  17.7 us (15%)
  waiting for transfers between devices  6.55 us (6%)
  other arithmetic  1.69 us (1%)
    ppermute x12, starting transfers between devices, body(): blocks[xh] = lax.ppermute(block, INST, along)  33.6 us
    ppermute x1, starting transfers between devices, body(): return call_merge(own, lax.ppermute(sib, INST, sibling))  16.1 us
    pallas_call x16, Pallas kernels, call_absorb(): pl.pallas_call(functools.partial(absorb_step, step, which), out_shape=(ST...  14.8 us
    ppermute x2, starting transfers between devices, body(): blocks = [lax.ppermute(block, INST, along) for block in blocks]  11.9 us
    all_to_all x1, starting transfers between devices, body(): lax.all_to_all(pre, ('xh', 'core', 'tp'), split_axis=0, concat_axis=0, ti...  10.4 us
    ppermute x3, starting transfers between devices, body(): lax.ppermute(span, INST, way)  9.36 us
    ppermute x1, starting transfers between devices, body(): mine = lax.ppermute(mine, INST, along)  4.01 us
    ppermute x12, waiting for transfers between devices, body(): blocks[xh] = lax.ppermute(block, INST, along)  2.35 us
  transfers between devices with their start and end apart: 21, of which 4 were waited for; matrix products, arithmetic and copies ran while one was open for 1% of the time, Pallas kernels for 14%

commit v1 on v0

--- a/solution.py
+++ b/solution.py
@@ -19,9 +19,9 @@
 CHIPS = XH * Z
 INST = ("xh", "z", "core")
 ROWS = SPAN // (CHIPS * CORE)
-KEYS = ROWS * CORE
-PIECE = PREFIX // CHIPS
-BLOCK_KEYS = KEYS + PIECE
+KEYS = ROWS * XH
+PIECE = PREFIX // (CHIPS * CORE)
+BLOCK_KEYS = KEYS + XH * PIECE
 LANES = 2 * ROWS
 PARTS = GROUP * ROWS // LANES
 STEPS = Z // 2
@@ -38,20 +38,13 @@
     return tile.astype(jnp.float32).T.astype(jnp.bfloat16)
 
 
-def pack(place_ref, own_ref, sib_ref, across_ref, diagonal_ref, pre_ref, *block_refs):
-    same_xh = [place_ref[0] == xh for xh in range(XH)]
-    same_core = [place_ref[2] == core for core in range(CORE)]
+def pack(place_ref, own_ref, across_ref, pre_ref, block_ref):
     for xh in range(XH):
-        for core in range(CORE):
-            tiles = []
-            for i in range(2):
-                near = jnp.where(same_core[core], own_ref[i], sib_ref[i])
-                far = jnp.where(same_core[core], across_ref[i], diagonal_ref[i])
-                tiles.append(jnp.where(same_xh[xh], near, far))
-            block_refs[xh][core * ROWS : (core + 1) * ROWS, :] = tiles[0]
-            block_refs[xh][BLOCK_KEYS + core * HD : BLOCK_KEYS + (core + 1) * HD, :] = turn(tiles[1])
-        block_refs[xh][KEYS:BLOCK_KEYS, :] = pre_ref[xh * PIECE : (xh + 1) * PIECE, :HD]
-        block_refs[xh][BLOCK_KEYS + KEYS :, :] = turn(pre_ref[xh * PIECE : (xh + 1) * PIECE, HD:])
+        tiles = [jnp.where(place_ref[0] == xh, own_ref[i], across_ref[i]) for i in range(2)]
+        block_ref[xh * ROWS : (xh + 1) * ROWS, :] = tiles[0]
+        block_ref[BLOCK_KEYS + xh * HD : BLOCK_KEYS + (xh + 1) * HD, :] = turn(tiles[1])
+    block_ref[KEYS:BLOCK_KEYS, :] = pre_ref[:, :HD]
+    block_ref[BLOCK_KEYS + KEYS :, :] = turn(pre_ref[:, HD:])
 
 
 def plan(place_ref, lengths_ref, seg_ref, q_ref, sib_ref, scalars_ref, bounds_ref, rows_ref):
@@ -98,11 +91,10 @@
             rows_ref[half, h // 2, :, h % 2 * ROWS : (h % 2 + 1) * ROWS] = turn(ref[:, h * HD : (h + 1) * HD])
 
 
-def absorb_step(step, which, place_ref, scalars_ref, bounds_ref, rows_ref, block_ref, *refs):
+def absorb_step(step, turned, final, place_ref, scalars_ref, bounds_ref, rows_ref, block_ref, *refs):
     core, z = place_ref[2], place_ref[1]
-    origin = lax.rem(jnp.where(core == 0, z - step + Z, z + step), Z)
-    xh = core if which is None else which
-    final = step == STEPS
+    upward = (core == 1) if turned else (core == 0)
+    origin = lax.rem(jnp.where(upward, z - step + Z, z + step), Z)
     if final:
         _, state, own_ref, sib_ref = refs
     else:
@@ -112,7 +104,7 @@
         state[:, :, HD:, :] = jnp.zeros((CORE, PARTS, STATE_ROWS - HD, LANES), jnp.float32)
         state[:, :, HD : HD + 1, :] = jnp.full((CORE, PARTS, 1, LANES), LOW, jnp.float32)
 
-    def absorb(half, row, count, base, kind, masked):
+    def absorb(half, row, count, index, kind, masked):
         keys = block_ref[row : row + count, :]
         vals = jnp.concatenate(
             [block_ref[BLOCK_KEYS + i : BLOCK_KEYS + i + HD, :] for i in range(row, row + count, HD)], axis=1
@@ -120,7 +112,6 @@
         every = range(PARTS)
         scores = [jnp.dot(keys, rows_ref[half, b], preferred_element_type=jnp.float32) for b in every]
         if masked:
-            index = base + lax.broadcasted_iota(jnp.int32, (count, ROWS), 0)
             low = bounds_ref[half, 2 * kind : 2 * kind + 1, :]
             high = bounds_ref[half, 2 * kind + 1 : 2 * kind + 2, :]
             bias = jnp.where((index >= low) & (index < high), 0.0, LOW)
@@ -143,22 +134,32 @@
             state[half, b, HD : HD + 1, :] = new[b]
             state[half, b, HD + 1 : HD + 2, :] = total[b]
 
-    def visit(half, row, count, base, kind):
-        least_lo, most_hi, most_lo, least_hi = [scalars_ref[half * 8 + kind * 4 + i] for i in range(4)]
-        seen = (base < most_hi) & (base + count > least_lo)
-        whole = (base >= most_lo) & (base + count <= least_hi)
-
-        @pl.when(seen & whole)
+    def overlaps(half, base, count, kind):
+        return (base < scalars_ref[half * 8 + kind * 4 + 1]) & (base + count > scalars_ref[half * 8 + kind * 4])
+
+    offset = lax.broadcasted_iota(jnp.int32, (ROWS, ROWS), 0)
+
+    def one_half(half, carry):
+        for xh in range(XH):
+            base = ((xh * Z + origin) * CORE + core) * ROWS
+            seen = overlaps(half, base, ROWS, 1)
+            whole = (base >= scalars_ref[half * 8 + 6]) & (base + ROWS <= scalars_ref[half * 8 + 7])
+
+            @pl.when(seen & whole)
+            def _():
+                absorb(half, xh * ROWS, ROWS, None, 1, False)
+
+            @pl.when(seen & jnp.logical_not(whole))
+            def _():
+                absorb(half, xh * ROWS, ROWS, base + offset, 1, True)
+
+        base = (origin * CORE + core) * PIECE
+        apart = PREFIX // XH
+
+        @pl.when(overlaps(half, base, PIECE, 0) | overlaps(half, base + apart, PIECE, 0))
         def _():
-            absorb(half, row, count, base, kind, False)
-
-        @pl.when(seen & jnp.logical_not(whole))
-        def _():
-            absorb(half, row, count, base, kind, True)
-
-    def one_half(half, carry):
-        visit(half, 0, KEYS, (xh * Z + origin) * KEYS, 1)
-        visit(half, KEYS, PIECE, (xh * Z + origin) * PIECE, 0)
+            absorb(half, KEYS, XH * PIECE, base + offset + jnp.where(offset >= PIECE, apart - PIECE, 0), 0, True)
+
         return carry
 
     lax.fori_loop(0, CORE, one_half, 0)
@@ -187,9 +188,9 @@
 def call_pack(place, *parts):
     return pl.pallas_call(
         pack,
-        out_shape=(jax.ShapeDtypeStruct((2 * BLOCK_KEYS, HD), jnp.bfloat16),) * XH,
-        in_specs=[SMEM] + [VMEM] * 5,
-        out_specs=(VMEM,) * XH,
+        out_shape=jax.ShapeDtypeStruct((2 * BLOCK_KEYS, HD), jnp.bfloat16),
+        in_specs=[SMEM] + [VMEM] * 3,
+        out_specs=VMEM,
         compiler_params=PARAMS,
         name="pack",
     )(place, *parts)
@@ -210,10 +211,10 @@
     )(place, prefix_lengths, span_seg.reshape(-1, ROWS), queries, sib_queries)
 
 
-def call_absorb(step, which, place, planned, block, state):
+def call_absorb(step, turned, place, planned, block, state):
     final = step == STEPS
     return pl.pallas_call(
-        functools.partial(absorb_step, step, which),
+        functools.partial(absorb_step, step, turned, final),
         out_shape=(STATE, HALF_STATE, HALF_STATE) if final else STATE,
         in_specs=[SMEM, SMEM, VMEM, VMEM, VMEM] + ([VMEM] if step else []),
         out_specs=(VMEM,) * 3 if final else VMEM,
@@ -244,36 +245,28 @@
     everyone = [(xh, z, c) for xh in range(XH) for z in range(Z) for c in range(CORE)]
     sibling = [(at(xh, z, c), at(xh, z, 1 - c)) for xh, z, c in everyone]
     across = [(at(xh, z, c), at(1 - xh, z, c)) for xh, z, c in everyone]
-    diagonal = [(at(xh, z, c), at(1 - xh, z, 1 - c)) for xh, z, c in everyone]
-    along = [(at(xh, z, c), at(xh, (z + 1 - 2 * c) % Z, c)) for xh, z, c in everyone]
+    ways = [[(at(xh, z, c), at(xh, (z + sign * (1 - 2 * c)) % Z, c)) for xh, z, c in everyone] for sign in (1, -1)]
 
     pre = jnp.concatenate(
         [prefix_keys.reshape(-1, KV_HEADS, HD), prefix_values.reshape(-1, KV_HEADS, HD)], axis=2
     ).transpose(1, 0, 2)
-    pre = jnp.broadcast_to(pre[None], (XH * CORE,) + pre.shape).reshape((XH * CORE * TP,) + pre.shape[1:])
-    pre = lax.all_to_all(pre, ("xh", "core", "tp"), split_axis=0, concat_axis=0, tiled=True)
+    pre = jnp.broadcast_to(pre[None], (XH,) + pre.shape).reshape((XH * TP,) + pre.shape[1:])
+    pre = lax.all_to_all(pre, ("xh", "tp"), split_axis=0, concat_axis=0, tiled=True)
     pre = pre.reshape(XH * PIECE, 2 * HD)
 
     span = jnp.stack([span_keys, span_values])
-    spans = [span] + [lax.ppermute(span, INST, way) for way in (sibling, across, diagonal)]
-    blocks = list(call_pack(place, *spans, pre))
+    held = call_pack(place, span, lax.ppermute(span, INST, across), pre)
     planned = call_plan(place, prefix_lengths, span_seg, queries, lax.ppermute(queries, INST, sibling))
 
-    mine = jnp.where(place[2] == 0, blocks[0], blocks[1])
-    blocks = [lax.ppermute(block, INST, along) for block in blocks]
-    state = call_absorb(0, None, place, planned, mine, None)
+    blocks = [lax.ppermute(held, INST, way) for way in ways]
+    state = call_absorb(0, False, place, planned, held, None)
     for step in range(1, STEPS):
-        for xh in range(XH):
-            block, state = lax.optimization_barrier((blocks[xh], state))
-            if step < STEPS - 1:
-                blocks[xh] = lax.ppermute(block, INST, along)
-            elif xh == 0:
-                blocks[xh] = block
-            else:
-                mine = jnp.where(place[2] == 0, blocks[0], block)
-                mine = lax.ppermute(mine, INST, along)
-            state = call_absorb(step, xh, place, planned, block, state)
-    _, own, sib = call_absorb(STEPS, None, place, planned, *lax.optimization_barrier((mine, state)))
+        for i, way in enumerate(ways):
+            block, state = lax.optimization_barrier((blocks[i], state))
+            if step < STEPS - 1 or i == 0:
+                blocks[i] = lax.ppermute(block, INST, way)
+            state = call_absorb(step, i == 1, place, planned, block, state)
+    _, own, sib = call_absorb(STEPS, False, place, planned, *lax.optimization_barrier((blocks[0], state)))
     return call_merge(own, lax.ppermute(sib, INST, sibling))
 
 

time: 115 us -> 117 us (1.017)
  Pallas kernels: 17.7 us -> 29.4 us
  starting transfers between devices: 87.4 us -> 79.1 us
  waiting for transfers between devices: 6.55 us -> 2.18 us
  local copies, waits for them, and re-layouts: 0.68 us -> 2.99 us
    pallas_call x17, Pallas kernels: 15.5 us -> 27.2 us  [the longest x16 26.5 us: call_absorb(): pl.pallas_call(functools.partial(absorb_step, step, turned, final), out_s...]
    ppermute x1, starting transfers between devices: 16.1 us -> 7.66 us  [body(): return call_merge(own, lax.ppermute(sib, INST, sibling))]
    ppermute x18 -> x16, waiting for transfers between devices: 4.99 us -> 0.61 us  [the longest x13 0.6 us: body(): blocks[i] = lax.ppermute(block, INST, way)]
    ppermute x1, starting transfers between devices: 1.98 us -> 5.19 us  [body(): lax.ppermute(queries, INST, sibling)]
    all_to_all x1, starting transfers between devices: 10.4 us -> 7.58 us  [body(): lax.all_to_all(pre, ('xh', 'tp'), split_axis=0, concat_axis=0, tiled=True)]
    unnamed x6, local copies, waits for them, and re-layouts: 0.01 us -> 2.36 us
    ppermute x18 -> x16, starting transfers between devices: 58.9 us -> 58.7 us  [the longest x13 42.7 us: body(): blocks[i] = lax.ppermute(block, INST, way)]
  transfers between devices with their start and end apart: 21 -> 19, of which waited for: 4 -> 2; matrix products, arithmetic and copies ran while one was open for 1% -> 1% of each run, Pallas kernels for 14% -> 23%
where the time goes in v1:
time: 117 us; the launch traced here: 116 us
  starting transfers between devices  79.1 us (68%)
  Pallas kernels  29.4 us (25%)
  local copies, waits for them, and re-layouts  2.99 us (3%)
  waiting for transfers between devices  2.18 us (2%)
  other arithmetic  1.6 us (1%)
    ppermute x13, starting transfers between devices, body(): blocks[i] = lax.ppermute(block, INST, way)  42.7 us
    pallas_call x16, Pallas kernels, call_absorb(): pl.pallas_call(functools.partial(absorb_step, step, turned, final), out_s...  26.5 us
    ppermute x2, starting transfers between devices, body(): blocks = [lax.ppermute(held, INST, way) for way in ways]  11.3 us
    ppermute x1, starting transfers between devices, body(): return call_merge(own, lax.ppermute(sib, INST, sibling))  7.66 us
    all_to_all x1, starting transfers between devices, body(): lax.all_to_all(pre, ('xh', 'tp'), split_axis=0, concat_axis=0, tiled=True)  7.58 us
    ppermute x1, starting transfers between devices, body(): lax.ppermute(queries, INST, sibling)  5.19 us
    ppermute x1, starting transfers between devices, body(): held = call_pack(place, span, lax.ppermute(span, INST, across), pre)  4.77 us
    unnamed x6, local copies, waits for them, and re-layouts  2.36 us
  transfers between devices with their start and end apart: 19, of which 2 were waited for; matrix products, arithmetic and copies ran while one was open for 1% of the time, Pallas kernels for 23%

profile of v1, /device:TPU:1, one launch (start us, length us, event | category | flops | bytes accessed | tf_op | source)
XLA Modules:
  0.0 115.7 jit_solution(2232891377963498898)
XLA Ops:
  1.4 7.6 %all-to-all-start = ((bf16[16,8,256]{2,1,0:T(8,128)(2,1)}), bf16[16,8,256]{2,1,0:T(8,128)(2,1)S(1)}, u32[]{:S(2)}, u32[]{:S(2)}) async-start(bf16[16,8,256]{2,1,0:T(8,128)(2,1)} %bitcast.9), calls=%async_computation | async-start | bytes 131072 | tf_op jit(solution)/shard_map/all_to_all | solution.py:254
  9.8 4.8 %collective-permute-start.1 = (bf16[2,128,128]{2,1,0:T(8,128)(2,1)S(1)}, bf16[2,128,128]{2,1,0:T(8,128)(2,1)S(1)}, u32[]{:S(2)}, u32[]{:S(2)}) collective-permute-start(bf16[2,128,128]{2,1,0:T(8,128)(2,1)S(1)} %pad_maximum_fusion.own_ref), channel_id=1, source_target_pairs={{0,256},{8,264},{16,272},{24,280},{32,288},{40,296},{48,304},{56,3... | collective-permute-start | bytes 196616 | tf_op jit(solution)/shard_map/ppermute | solution.py:258
  14.5 5.2 %collective-permute-start = (bf16[128,1024]{1,0:T(8,128)(2,1)}, bf16[128,1024]{1,0:T(8,128)(2,1)S(1)}, u32[]{:S(2)}, u32[]{:S(2)}) collective-permute-start(bf16[128,1024]{1,0:T(8,128)(2,1)} %q_ref.1), channel_id=1, source_target_pairs={{0,8},{8,0},{16,24},{24,16},{32,40},{40,32},{48,56},{56,48},{64,72... | collective-permute-start | bytes 786440 | tf_op jit(solution)/shard_map/ppermute | solution.py:259
  20.5 9.4 %collective-permute-start.2 = (bf16[768,128]{1,0:T(8,128)(2,1)S(1)}, bf16[768,128]{1,0:T(8,128)(2,1)S(1)}, u32[]{:S(2)}, u32[]{:S(2)}) collective-permute-start(bf16[768,128]{1,0:T(8,128)(2,1)S(1)} %pack.1.block_ref), channel_id=1, source_target_pairs={{0,16},{8,248},{16,32},{24,8},{32,48},{40,24},{48,64},{56,40},{64,... | collective-permute-start | bytes 589832 | tf_op jit(solution)/shard_map/ppermute | solution.py:261
  29.8 1.9 %collective-permute-start.4 = (bf16[768,128]{1,0:T(8,128)(2,1)S(1)}, bf16[768,128]{1,0:T(8,128)(2,1)S(1)}, u32[]{:S(2)}, u32[]{:S(2)}) collective-permute-start(bf16[768,128]{1,0:T(8,128)(2,1)S(1)} %pack.1.block_ref), channel_id=1, source_target_pairs={{0,240},{8,24},{16,0},{24,40},{32,16},{40,56},{48,32},{56,72},{64,... | collective-permute-start | bytes 589832 | tf_op jit(solution)/shard_map/ppermute | solution.py:261
  35.5 2.2 %absorb.16.refs_0_ = f32[2,4,136,256]{3,2,1,0:T(8,128)S(1)} custom-call(s32[3]{0:T(128)S(1)} %pad_add_fusion.place_ref, s32[16]{0:T(128)S(1)} %get-tuple-element.40.scalars_ref, s32[2,8,128]{2,1,0:T(8,128)S(1)} %get-tuple-element.41.bounds_ref, bf16[2,4,128,256]{3,2,1,0:T(8,128)(2,1)S(1)} %get-tuple-element.42.rows_ref, bf16[768,128]{1,0:T(8,128)(2,1)S(1)} %pack.1.block_ref), custom_call_target="tpu_custom_call" | custom-call | flops 400000000 | bytes 2000000 | tf_op jit(solution)/shard_map/absorb/pallas_call | solution.py:216
  37.6 3.6 %collective-permute-start.3 = (bf16[768,128]{1,0:T(8,128)(2,1)S(1)}, bf16[768,128]{1,0:T(8,128)(2,1)S(1)}, u32[]{:S(2)}, u32[]{:S(2)}) collective-permute-start(bf16[768,128]{1,0:T(8,128)(2,1)S(1)} %collective-permute-done.2.block_ref), channel_id=1, source_target_pairs={{0,16},{8,248},{16,32},{24,8},{32,48},{40,24},{48,64},{56,40},{64,... | collective-permute-start | bytes 589832 | tf_op jit(solution)/shard_map/ppermute | solution.py:267
  42.9 1.9 %collective-permute-start.6 = (bf16[768,128]{1,0:T(8,128)(2,1)S(1)}, bf16[768,128]{1,0:T(8,128)(2,1)S(1)}, u32[]{:S(2)}, u32[]{:S(2)}) collective-permute-start(bf16[768,128]{1,0:T(8,128)(2,1)S(1)} %collective-permute-done.4.block_ref), channel_id=1, source_target_pairs={{0,240},{8,24},{16,0},{24,40},{32,16},{40,56},{48,32},{56,72},{64,... | collective-permute-start | bytes 589832 | tf_op jit(solution)/shard_map/ppermute | solution.py:267
  44.8 1.6 %absorb.18.refs_0_ = f32[2,4,136,256]{3,2,1,0:T(8,128)S(1)} custom-call(s32[3]{0:T(128)S(1)} %pad_add_fusion.place_ref, s32[16]{0:T(128)S(1)} %get-tuple-element.40.scalars_ref, s32[2,8,128]{2,1,0:T(8,128)S(1)} %get-tuple-element.41.bounds_ref, bf16[2,4,128,256]{3,2,1,0:T(8,128)(2,1)S(1)} %get-tuple-element.42.rows_ref, ...), custom_call_target="tpu_custom_call", output_to_operand_aliasing={{}: (5, {})} | custom-call | flops 400000000 | bytes 2000000 | tf_op jit(solution)/shard_map/absorb/pallas_call | solution.py:216
  46.5 4.5 %collective-permute-start.5 = (bf16[768,128]{1,0:T(8,128)(2,1)S(1)}, bf16[768,128]{1,0:T(8,128)(2,1)S(1)}, u32[]{:S(2)}, u32[]{:S(2)}) collective-permute-start(bf16[768,128]{1,0:T(8,128)(2,1)S(1)} %collective-permute-done.3.block_ref), channel_id=1, source_target_pairs={{0,16},{8,248},{16,32},{24,8},{32,48},{40,24},{48,64},{56,40},{64,... | collective-permute-start | bytes 589832 | tf_op jit(solution)/shard_map/ppermute | solution.py:267
  52.6 1.9 %collective-permute-start.8 = (bf16[768,128]{1,0:T(8,128)(2,1)S(1)}, bf16[768,128]{1,0:T(8,128)(2,1)S(1)}, u32[]{:S(2)}, u32[]{:S(2)}) collective-permute-start(bf16[768,128]{1,0:T(8,128)(2,1)S(1)} %collective-permute-done.6.block_ref), channel_id=1, source_target_pairs={{0,240},{8,24},{16,0},{24,40},{32,16},{40,56},{48,32},{56,72},{64,... | collective-permute-start | bytes 589832 | tf_op jit(solution)/shard_map/ppermute | solution.py:267
  54.6 1.6 %absorb.20.refs_0_ = f32[2,4,136,256]{3,2,1,0:T(8,128)S(1)} custom-call(s32[3]{0:T(128)S(1)} %pad_add_fusion.place_ref, s32[16]{0:T(128)S(1)} %get-tuple-element.40.scalars_ref, s32[2,8,128]{2,1,0:T(8,128)S(1)} %get-tuple-element.41.bounds_ref, bf16[2,4,128,256]{3,2,1,0:T(8,128)(2,1)S(1)} %get-tuple-element.42.rows_ref, ...), custom_call_target="tpu_custom_call", output_to_operand_aliasing={{}: (5, {})} | custom-call | flops 400000000 | bytes 2000000 | tf_op jit(solution)/shard_map/absorb/pallas_call | solution.py:216
  56.2 4.5 %collective-permute-start.7 = (bf16[768,128]{1,0:T(8,128)(2,1)S(1)}, bf16[768,128]{1,0:T(8,128)(2,1)S(1)}, u32[]{:S(2)}, u32[]{:S(2)}) collective-permute-start(bf16[768,128]{1,0:T(8,128)(2,1)S(1)} %collective-permute-done.5.block_ref), channel_id=1, source_target_pairs={{0,16},{8,248},{16,32},{24,8},{32,48},{40,24},{48,64},{56,40},{64,... | collective-permute-start | bytes 589832 | tf_op jit(solution)/shard_map/ppermute | solution.py:267
  60.7 1.6 %absorb.21.refs_0_ = f32[2,4,136,256]{3,2,1,0:T(8,128)S(1)} custom-call(s32[3]{0:T(128)S(1)} %pad_add_fusion.place_ref, s32[16]{0:T(128)S(1)} %get-tuple-element.40.scalars_ref, s32[2,8,128]{2,1,0:T(8,128)S(1)} %get-tuple-element.41.bounds_ref, bf16[2,4,128,256]{3,2,1,0:T(8,128)(2,1)S(1)} %get-tuple-element.42.rows_ref, ...), custom_call_target="tpu_custom_call", output_to_operand_aliasing={{}: (5, {})} | custom-call | flops 400000000 | bytes 2000000 | tf_op jit(solution)/shard_map/absorb/pallas_call | solution.py:216
  62.4 2.1 %collective-permute-start.10 = (bf16[768,128]{1,0:T(8,128)(2,1)S(1)}, bf16[768,128]{1,0:T(8,128)(2,1)S(1)}, u32[]{:S(2)}, u32[]{:S(2)}) collective-permute-start(bf16[768,128]{1,0:T(8,128)(2,1)S(1)} %collective-permute-done.8.block_ref), channel_id=1, source_target_pairs={{0,240},{8,24},{16,0},{24,40},{32,16},{40,56},{48,32},{56,72},{64,... | collective-permute-start | bytes 589832 | tf_op jit(solution)/shard_map/ppermute | solution.py:267
  64.5 1.6 %absorb.22.refs_0_ = f32[2,4,136,256]{3,2,1,0:T(8,128)S(1)} custom-call(s32[3]{0:T(128)S(1)} %pad_add_fusion.place_ref, s32[16]{0:T(128)S(1)} %get-tuple-element.40.scalars_ref, s32[2,8,128]{2,1,0:T(8,128)S(1)} %get-tuple-element.41.bounds_ref, bf16[2,4,128,256]{3,2,1,0:T(8,128)(2,1)S(1)} %get-tuple-element.42.rows_ref, ...), custom_call_target="tpu_custom_call", output_to_operand_aliasing={{}: (5, {})} | custom-call | flops 400000000 | bytes 2000000 | tf_op jit(solution)/shard_map/absorb/pallas_call | solution.py:216
  66.1 4.5 %collective-permute-start.9 = (bf16[768,128]{1,0:T(8,128)(2,1)S(1)}, bf16[768,128]{1,0:T(8,128)(2,1)S(1)}, u32[]{:S(2)}, u32[]{:S(2)}) collective-permute-start(bf16[768,128]{1,0:T(8,128)(2,1)S(1)} %collective-permute-done.7.block_ref), channel_id=1, source_target_pairs={{0,16},{8,248},{16,32},{24,8},{32,48},{40,24},{48,64},{56,40},{64,... | collective-permute-start | bytes 589832 | tf_op jit(solution)/shard_map/ppermute | solution.py:267
  70.6 1.6 %absorb.23.refs_0_ = f32[2,4,136,256]{3,2,1,0:T(8,128)S(1)} custom-call(s32[3]{0:T(128)S(1)} %pad_add_fusion.place_ref, s32[16]{0:T(128)S(1)} %get-tuple-element.40.scalars_ref, s32[2,8,128]{2,1,0:T(8,128)S(1)} %get-tuple-element.41.bounds_ref, bf16[2,4,128,256]{3,2,1,0:T(8,128)(2,1)S(1)} %get-tuple-element.42.rows_ref, ...), custom_call_target="tpu_custom_call", output_to_operand_aliasing={{}: (5, {})} | custom-call | flops 400000000 | bytes 2000000 | tf_op jit(solution)/shard_map/absorb/pallas_call | solution.py:216
  72.3 1.9 %collective-permute-start.12 = (bf16[768,128]{1,0:T(8,128)(2,1)S(1)}, bf16[768,128]{1,0:T(8,128)(2,1)S(1)}, u32[]{:S(2)}, u32[]{:S(2)}) collective-permute-start(bf16[768,128]{1,0:T(8,128)(2,1)S(1)} %collective-permute-done.10.block_ref), channel_id=1, source_target_pairs={{0,240},{8,24},{16,0},{24,40},{32,16},{40,56},{48,32},{56,72},{64,... | collective-permute-start | bytes 589832 | tf_op jit(solution)/shard_map/ppermute | solution.py:267
  74.2 1.6 %absorb.24.refs_0_ = f32[2,4,136,256]{3,2,1,0:T(8,128)S(1)} custom-call(s32[3]{0:T(128)S(1)} %pad_add_fusion.place_ref, s32[16]{0:T(128)S(1)} %get-tuple-element.40.scalars_ref, s32[2,8,128]{2,1,0:T(8,128)S(1)} %get-tuple-element.41.bounds_ref, bf16[2,4,128,256]{3,2,1,0:T(8,128)(2,1)S(1)} %get-tuple-element.42.rows_ref, ...), custom_call_target="tpu_custom_call", output_to_operand_aliasing={{}: (5, {})} | custom-call | flops 400000000 | bytes 2000000 | tf_op jit(solution)/shard_map/absorb/pallas_call | solution.py:216
  75.8 4.5 %collective-permute-start.11 = (bf16[768,128]{1,0:T(8,128)(2,1)S(1)}, bf16[768,128]{1,0:T(8,128)(2,1)S(1)}, u32[]{:S(2)}, u32[]{:S(2)}) collective-permute-start(bf16[768,128]{1,0:T(8,128)(2,1)S(1)} %collective-permute-done.9.block_ref), channel_id=1, source_target_pairs={{0,16},{8,248},{16,32},{24,8},{32,48},{40,24},{48,64},{56,40},{64,... | collective-permute-start | bytes 589832 | tf_op jit(solution)/shard_map/ppermute | solution.py:267
  80.4 1.6 %absorb.25.refs_0_ = f32[2,4,136,256]{3,2,1,0:T(8,128)S(1)} custom-call(s32[3]{0:T(128)S(1)} %pad_add_fusion.place_ref, s32[16]{0:T(128)S(1)} %get-tuple-element.40.scalars_ref, s32[2,8,128]{2,1,0:T(8,128)S(1)} %get-tuple-element.41.bounds_ref, bf16[2,4,128,256]{3,2,1,0:T(8,128)(2,1)S(1)} %get-tuple-element.42.rows_ref, ...), custom_call_target="tpu_custom_call", output_to_operand_aliasing={{}: (5, {})} | custom-call | flops 400000000 | bytes 2000000 | tf_op jit(solution)/shard_map/absorb/pallas_call | solution.py:216
  82.0 1.9 %collective-permute-start.14 = (bf16[768,128]{1,0:T(8,128)(2,1)S(1)}, bf16[768,128]{1,0:T(8,128)(2,1)S(1)}, u32[]{:S(2)}, u32[]{:S(2)}) collective-permute-start(bf16[768,128]{1,0:T(8,128)(2,1)S(1)} %collective-permute-done.12.block_ref), channel_id=1, source_target_pairs={{0,240},{8,24},{16,0},{24,40},{32,16},{40,56},{48,32},{56,72},{64,... | collective-permute-start | bytes 589832 | tf_op jit(solution)/shard_map/ppermute | solution.py:267
  83.9 1.6 %absorb.26.refs_0_ = f32[2,4,136,256]{3,2,1,0:T(8,128)S(1)} custom-call(s32[3]{0:T(128)S(1)} %pad_add_fusion.place_ref, s32[16]{0:T(128)S(1)} %get-tuple-element.40.scalars_ref, s32[2,8,128]{2,1,0:T(8,128)S(1)} %get-tuple-element.41.bounds_ref, bf16[2,4,128,256]{3,2,1,0:T(8,128)(2,1)S(1)} %get-tuple-element.42.rows_ref, ...), custom_call_target="tpu_custom_call", output_to_operand_aliasing={{}: (5, {})} | custom-call | flops 400000000 | bytes 2000000 | tf_op jit(solution)/shard_map/absorb/pallas_call | solution.py:216
  85.6 4.5 %collective-permute-start.13 = (bf16[768,128]{1,0:T(8,128)(2,1)S(1)}, bf16[768,128]{1,0:T(8,128)(2,1)S(1)}, u32[]{:S(2)}, u32[]{:S(2)}) collective-permute-start(bf16[768,128]{1,0:T(8,128)(2,1)S(1)} %collective-permute-done.11.block_ref), channel_id=1, source_target_pairs={{0,16},{8,248},{16,32},{24,8},{32,48},{40,24},{48,64},{56,40},{64,... | collective-permute-start | bytes 589832 | tf_op jit(solution)/shard_map/ppermute | solution.py:267
  90.1 1.6 %absorb.27.refs_0_ = f32[2,4,136,256]{3,2,1,0:T(8,128)S(1)} custom-call(s32[3]{0:T(128)S(1)} %pad_add_fusion.place_ref, s32[16]{0:T(128)S(1)} %get-tuple-element.40.scalars_ref, s32[2,8,128]{2,1,0:T(8,128)S(1)} %get-tuple-element.41.bounds_ref, bf16[2,4,128,256]{3,2,1,0:T(8,128)(2,1)S(1)} %get-tuple-element.42.rows_ref, ...), custom_call_target="tpu_custom_call", output_to_operand_aliasing={{}: (5, {})} | custom-call | flops 400000000 | bytes 2000000 | tf_op jit(solution)/shard_map/absorb/pallas_call | solution.py:216
  91.7 2.1 %collective-permute-start.16 = (bf16[768,128]{1,0:T(8,128)(2,1)S(1)}, bf16[768,128]{1,0:T(8,128)(2,1)S(1)}, u32[]{:S(2)}, u32[]{:S(2)}) collective-permute-start(bf16[768,128]{1,0:T(8,128)(2,1)S(1)} %collective-permute-done.14.block_ref), channel_id=1, source_target_pairs={{0,240},{8,24},{16,0},{24,40},{32,16},{40,56},{48,32},{56,72},{64,... | collective-permute-start | bytes 589832 | tf_op jit(solution)/shard_map/ppermute | solution.py:267
  93.9 1.6 %absorb.28.refs_0_ = f32[2,4,136,256]{3,2,1,0:T(8,128)S(1)} custom-call(s32[3]{0:T(128)S(1)} %pad_add_fusion.place_ref, s32[16]{0:T(128)S(1)} %get-tuple-element.40.scalars_ref, s32[2,8,128]{2,1,0:T(8,128)S(1)} %get-tuple-element.41.bounds_ref, bf16[2,4,128,256]{3,2,1,0:T(8,128)(2,1)S(1)} %get-tuple-element.42.rows_ref, ...), custom_call_target="tpu_custom_call", output_to_operand_aliasing={{}: (5, {})} | custom-call | flops 400000000 | bytes 2000000 | tf_op jit(solution)/shard_map/absorb/pallas_call | solution.py:216
  95.5 4.5 %collective-permute-start.15 = (bf16[768,128]{1,0:T(8,128)(2,1)S(1)}, bf16[768,128]{1,0:T(8,128)(2,1)S(1)}, u32[]{:S(2)}, u32[]{:S(2)}) collective-permute-start(bf16[768,128]{1,0:T(8,128)(2,1)S(1)} %collective-permute-done.13.block_ref), channel_id=1, source_target_pairs={{0,16},{8,248},{16,32},{24,8},{32,48},{40,24},{48,64},{56,40},{64,... | collective-permute-start | bytes 589832 | tf_op jit(solution)/shard_map/ppermute | solution.py:267
  101.7 1.6 %absorb.30.refs_0_ = f32[2,4,136,256]{3,2,1,0:T(8,128)S(1)} custom-call(s32[3]{0:T(128)S(1)} %pad_add_fusion.place_ref, s32[16]{0:T(128)S(1)} %get-tuple-element.40.scalars_ref, s32[2,8,128]{2,1,0:T(8,128)S(1)} %get-tuple-element.41.bounds_ref, bf16[2,4,128,256]{3,2,1,0:T(8,128)(2,1)S(1)} %get-tuple-element.42.rows_ref, ...), custom_call_target="tpu_custom_call", output_to_operand_aliasing={{}: (5, {})} | custom-call | flops 400000000 | bytes 2000000 | tf_op jit(solution)/shard_map/absorb/pallas_call | solution.py:216
  103.9 1.7 %absorb.31 = (f32[2,4,136,256]{3,2,1,0:T(8,128)S(1)}, f32[4,136,256]{2,1,0:T(8,128)S(1)}, f32[4,136,256]{2,1,0:T(8,128)S(1)}) custom-call(s32[3]{0:T(128)S(1)} %pad_add_fusion.place_ref, s32[16]{0:T(128)S(1)} %get-tuple-element.40.scalars_ref, s32[2,8,128]{2,1,0:T(8,128)S(1)} %get-tuple-element.41.bounds_ref, ...), custom_call_target="tpu_custom_call", output_to_operand_aliasing={{0}: (5, {})} | custom-call | flops 400000000 | bytes 2000000 | tf_op jit(solution)/shard_map/absorb/pallas_call | solution.py:216
  105.6 7.7 %collective-permute-start.17 = (f32[4,136,256]{2,1,0:T(8,128)S(1)}, f32[4,136,256]{2,1,0:T(8,128)S(1)}, u32[]{:S(2)}, u32[]{:S(2)}) collective-permute-start(f32[4,136,256]{2,1,0:T(8,128)S(1)} %get-tuple-element.74), channel_id=1, source_target_pairs={{0,8},{8,0},{16,24},{24,16},{32,40},{40,32},{48,56},{56,48},{64,72... | collective-permute-start | bytes 1671176 | tf_op jit(solution)/shard_map/ppermute | solution.py:270
  (35 shorter events, 14.4 us)
Async XLA Ops:
  1.4 18.4 %all-to-all-start = ((bf16[16,8,256]{2,1,0:T(8,128)(2,1)}), bf16[16,8,256]{2,1,0:T(8,128)(2,1)S(1)}, u32[]{:S(2)}, u32[]{:S(2)}) async-start(bf16[16,8,256]{2,1,0:T(8,128)(2,1)} %bitcast.9), calls=%async_computation | async-start | bytes 131072 | tf_op jit(solution)/shard_map/all_to_all | solution.py:254
  9.8 10.1 %collective-permute-start.1 = (bf16[2,128,128]{2,1,0:T(8,128)(2,1)S(1)}, bf16[2,128,128]{2,1,0:T(8,128)(2,1)S(1)}, u32[]{:S(2)}, u32[]{:S(2)}) collective-permute-start(bf16[2,128,128]{2,1,0:T(8,128)(2,1)S(1)} %pad_maximum_fusion.own_ref), channel_id=1, source_target_pairs={{0,256},{8,264},{16,272},{24,280},{32,288},{40,296},{48,304},{56,3... | collective-permute-start | bytes 196616 | tf_op jit(solution)/shard_map/ppermute | solution.py:258
  14.5 17.2 %collective-permute-start = (bf16[128,1024]{1,0:T(8,128)(2,1)}, bf16[128,1024]{1,0:T(8,128)(2,1)S(1)}, u32[]{:S(2)}, u32[]{:S(2)}) collective-permute-start(bf16[128,1024]{1,0:T(8,128)(2,1)} %q_ref.1), channel_id=1, source_target_pairs={{0,8},{8,0},{16,24},{24,16},{32,40},{40,32},{48,56},{56,48},{64,72... | collective-permute-start | bytes 786440 | tf_op jit(solution)/shard_map/ppermute | solution.py:259
  20.5 17.2 %collective-permute-start.2 = (bf16[768,128]{1,0:T(8,128)(2,1)S(1)}, bf16[768,128]{1,0:T(8,128)(2,1)S(1)}, u32[]{:S(2)}, u32[]{:S(2)}) collective-permute-start(bf16[768,128]{1,0:T(8,128)(2,1)S(1)} %pack.1.block_ref), channel_id=1, source_target_pairs={{0,16},{8,248},{16,32},{24,8},{32,48},{40,24},{48,64},{56,40},{64,... | collective-permute-start | bytes 589832 | tf_op jit(solution)/shard_map/ppermute | solution.py:261
  29.8 13.0 %collective-permute-start.4 = (bf16[768,128]{1,0:T(8,128)(2,1)S(1)}, bf16[768,128]{1,0:T(8,128)(2,1)S(1)}, u32[]{:S(2)}, u32[]{:S(2)}) collective-permute-start(bf16[768,128]{1,0:T(8,128)(2,1)S(1)} %pack.1.block_ref), channel_id=1, source_target_pairs={{0,240},{8,24},{16,0},{24,40},{32,16},{40,56},{48,32},{56,72},{64,... | collective-permute-start | bytes 589832 | tf_op jit(solution)/shard_map/ppermute | solution.py:261
  31.8 1.0 copy-start
  32.7 0.8 copy-start.1
  33.5 0.7 copy-start.2
  37.6 8.8 %collective-permute-start.3 = (bf16[768,128]{1,0:T(8,128)(2,1)S(1)}, bf16[768,128]{1,0:T(8,128)(2,1)S(1)}, u32[]{:S(2)}, u32[]{:S(2)}) collective-permute-start(bf16[768,128]{1,0:T(8,128)(2,1)S(1)} %collective-permute-done.2.block_ref), channel_id=1, source_target_pairs={{0,16},{8,248},{16,32},{24,8},{32,48},{40,24},{48,64},{56,40},{64,... | collective-permute-start | bytes 589832 | tf_op jit(solution)/shard_map/ppermute | solution.py:267
  42.9 9.7 %collective-permute-start.6 = (bf16[768,128]{1,0:T(8,128)(2,1)S(1)}, bf16[768,128]{1,0:T(8,128)(2,1)S(1)}, u32[]{:S(2)}, u32[]{:S(2)}) collective-permute-start(bf16[768,128]{1,0:T(8,128)(2,1)S(1)} %collective-permute-done.4.block_ref), channel_id=1, source_target_pairs={{0,240},{8,24},{16,0},{24,40},{32,16},{40,56},{48,32},{56,72},{64,... | collective-permute-start | bytes 589832 | tf_op jit(solution)/shard_map/ppermute | solution.py:267
  46.5 9.7 %collective-permute-start.5 = (bf16[768,128]{1,0:T(8,128)(2,1)S(1)}, bf16[768,128]{1,0:T(8,128)(2,1)S(1)}, u32[]{:S(2)}, u32[]{:S(2)}) collective-permute-start(bf16[768,128]{1,0:T(8,128)(2,1)S(1)} %collective-permute-done.3.block_ref), channel_id=1, source_target_pairs={{0,16},{8,248},{16,32},{24,8},{32,48},{40,24},{48,64},{56,40},{64,... | collective-permute-start | bytes 589832 | tf_op jit(solution)/shard_map/ppermute | solution.py:267
  52.6 9.7 %collective-permute-start.8 = (bf16[768,128]{1,0:T(8,128)(2,1)S(1)}, bf16[768,128]{1,0:T(8,128)(2,1)S(1)}, u32[]{:S(2)}, u32[]{:S(2)}) collective-permute-start(bf16[768,128]{1,0:T(8,128)(2,1)S(1)} %collective-permute-done.6.block_ref), channel_id=1, source_target_pairs={{0,240},{8,24},{16,0},{24,40},{32,16},{40,56},{48,32},{56,72},{64,... | collective-permute-start | bytes 589832 | tf_op jit(solution)/shard_map/ppermute | solution.py:267
  56.2 9.9 %collective-permute-start.7 = (bf16[768,128]{1,0:T(8,128)(2,1)S(1)}, bf16[768,128]{1,0:T(8,128)(2,1)S(1)}, u32[]{:S(2)}, u32[]{:S(2)}) collective-permute-start(bf16[768,128]{1,0:T(8,128)(2,1)S(1)} %collective-permute-done.5.block_ref), channel_id=1, source_target_pairs={{0,16},{8,248},{16,32},{24,8},{32,48},{40,24},{48,64},{56,40},{64,... | collective-permute-start | bytes 589832 | tf_op jit(solution)/shard_map/ppermute | solution.py:267
  62.4 9.9 %collective-permute-start.10 = (bf16[768,128]{1,0:T(8,128)(2,1)S(1)}, bf16[768,128]{1,0:T(8,128)(2,1)S(1)}, u32[]{:S(2)}, u32[]{:S(2)}) collective-permute-start(bf16[768,128]{1,0:T(8,128)(2,1)S(1)} %collective-permute-done.8.block_ref), channel_id=1, source_target_pairs={{0,240},{8,24},{16,0},{24,40},{32,16},{40,56},{48,32},{56,72},{64,... | collective-permute-start | bytes 589832 | tf_op jit(solution)/shard_map/ppermute | solution.py:267
  66.1 9.7 %collective-permute-start.9 = (bf16[768,128]{1,0:T(8,128)(2,1)S(1)}, bf16[768,128]{1,0:T(8,128)(2,1)S(1)}, u32[]{:S(2)}, u32[]{:S(2)}) collective-permute-start(bf16[768,128]{1,0:T(8,128)(2,1)S(1)} %collective-permute-done.7.block_ref), channel_id=1, source_target_pairs={{0,16},{8,248},{16,32},{24,8},{32,48},{40,24},{48,64},{56,40},{64,... | collective-permute-start | bytes 589832 | tf_op jit(solution)/shard_map/ppermute | solution.py:267
  72.3 9.7 %collective-permute-start.12 = (bf16[768,128]{1,0:T(8,128)(2,1)S(1)}, bf16[768,128]{1,0:T(8,128)(2,1)S(1)}, u32[]{:S(2)}, u32[]{:S(2)}) collective-permute-start(bf16[768,128]{1,0:T(8,128)(2,1)S(1)} %collective-permute-done.10.block_ref), channel_id=1, source_target_pairs={{0,240},{8,24},{16,0},{24,40},{32,16},{40,56},{48,32},{56,72},{64,... | collective-permute-start | bytes 589832 | tf_op jit(solution)/shard_map/ppermute | solution.py:267
  75.8 9.7 %collective-permute-start.11 = (bf16[768,128]{1,0:T(8,128)(2,1)S(1)}, bf16[768,128]{1,0:T(8,128)(2,1)S(1)}, u32[]{:S(2)}, u32[]{:S(2)}) collective-permute-start(bf16[768,128]{1,0:T(8,128)(2,1)S(1)} %collective-permute-done.9.block_ref), channel_id=1, source_target_pairs={{0,16},{8,248},{16,32},{24,8},{32,48},{40,24},{48,64},{56,40},{64,... | collective-permute-start | bytes 589832 | tf_op jit(solution)/shard_map/ppermute | solution.py:267
  82.0 9.7 %collective-permute-start.14 = (bf16[768,128]{1,0:T(8,128)(2,1)S(1)}, bf16[768,128]{1,0:T(8,128)(2,1)S(1)}, u32[]{:S(2)}, u32[]{:S(2)}) collective-permute-start(bf16[768,128]{1,0:T(8,128)(2,1)S(1)} %collective-permute-done.12.block_ref), channel_id=1, source_target_pairs={{0,240},{8,24},{16,0},{24,40},{32,16},{40,56},{48,32},{56,72},{64,... | collective-permute-start | bytes 589832 | tf_op jit(solution)/shard_map/ppermute | solution.py:267
  85.6 9.9 %collective-permute-start.13 = (bf16[768,128]{1,0:T(8,128)(2,1)S(1)}, bf16[768,128]{1,0:T(8,128)(2,1)S(1)}, u32[]{:S(2)}, u32[]{:S(2)}) collective-permute-start(bf16[768,128]{1,0:T(8,128)(2,1)S(1)} %collective-permute-done.11.block_ref), channel_id=1, source_target_pairs={{0,16},{8,248},{16,32},{24,8},{32,48},{40,24},{48,64},{56,40},{64,... | collective-permute-start | bytes 589832 | tf_op jit(solution)/shard_map/ppermute | solution.py:267
  91.7 9.9 %collective-permute-start.16 = (bf16[768,128]{1,0:T(8,128)(2,1)S(1)}, bf16[768,128]{1,0:T(8,128)(2,1)S(1)}, u32[]{:S(2)}, u32[]{:S(2)}) collective-permute-start(bf16[768,128]{1,0:T(8,128)(2,1)S(1)} %collective-permute-done.14.block_ref), channel_id=1, source_target_pairs={{0,240},{8,24},{16,0},{24,40},{32,16},{40,56},{48,32},{56,72},{64,... | collective-permute-start | bytes 589832 | tf_op jit(solution)/shard_map/ppermute | solution.py:267
  95.5 8.4 %collective-permute-start.15 = (bf16[768,128]{1,0:T(8,128)(2,1)S(1)}, bf16[768,128]{1,0:T(8,128)(2,1)S(1)}, u32[]{:S(2)}, u32[]{:S(2)}) collective-permute-start(bf16[768,128]{1,0:T(8,128)(2,1)S(1)} %collective-permute-done.13.block_ref), channel_id=1, source_target_pairs={{0,16},{8,248},{16,32},{24,8},{32,48},{40,24},{48,64},{56,40},{64,... | collective-permute-start | bytes 589832 | tf_op jit(solution)/shard_map/ppermute | solution.py:267
  105.6 9.2 %collective-permute-start.17 = (f32[4,136,256]{2,1,0:T(8,128)S(1)}, f32[4,136,256]{2,1,0:T(8,128)S(1)}, u32[]{:S(2)}, u32[]{:S(2)}) collective-permute-start(f32[4,136,256]{2,1,0:T(8,128)S(1)} %get-tuple-element.74), channel_id=1, source_target_pairs={{0,8},{8,0},{16,24},{24,16},{32,40},{40,32},{48,56},{56,48},{64,72... | collective-permute-start | bytes 1671176 | tf_op jit(solution)/shard_map/ppermute | solution.py:270
